TPU v7x, 256 devices: a whole 4x4x8 slice. The times are simulated.
256 devices in a mesh: row: 32 (over z, x), col: 8 (over y, core).
Axes of the slice: x: 4, y: 4, z: 8, core: 2. Of those that a mesh axis runs over, the one named last changes fastest.
Arguments:
- tokens: bfloat16 [2048, 4096], P('row', 'col'), may hold values from -6 to 6
- gate_weight: bfloat16 [4096, 14336], P('col', 'row'), may hold values from -0.09375 to 0.09375
- up_weight: bfloat16 [4096, 14336], P('col', 'row'), may hold values from -0.09375 to 0.09375
- down_weight: bfloat16 [14336, 4096], P('row', 'col'), may hold values from -0.046875 to 0.046875
- gate_mask: int32 [32, 112], replicated, may hold values 0 or 1
- up_mask: int32 [32, 112], replicated, may hold values 0 or 1
- down_mask: int32 [112, 32], replicated, may hold values 0 or 1
- out_grad: bfloat16 [2048, 4096], P('row', 'col'), may hold values from -6 to 6
Outputs:
- mixed: bfloat16 [2048, 4096], P('row', 'col')
- input_grad: bfloat16 [2048, 4096], P('row', 'col')
- gate_grad: float32 [4096, 14336], P('col', 'row')
- up_grad: float32 [4096, 14336], P('col', 'row')
- down_grad: float32 [14336, 4096], P('row', 'col')
All inputs are finite; a program needn't handle non-finite values.
Results may differ from a plain program's by a relative error of at most 0.0049.
Values may be sent and summed in bfloat16 or wider, within the bound.
A program may use at most 64 MiB of HBM per device.

v0:
```python
import jax
import jax.numpy as jnp
from jax import lax
from jax.sharding import PartitionSpec as P

BLOCK = 128


def expand_mask(mask, row_start, row_count, col_start, col_count):
    row_block = (row_start + lax.broadcasted_iota(jnp.int32, (row_count, 1), 0)) // BLOCK
    left = (row_block == lax.broadcasted_iota(jnp.int32, (1, mask.shape[0]), 1)).astype(jnp.float32)
    col_block = (col_start + lax.broadcasted_iota(jnp.int32, (1, col_count), 1)) // BLOCK
    right = (lax.broadcasted_iota(jnp.int32, (mask.shape[1], 1), 0) == col_block).astype(
        jnp.float32
    )
    middle = jnp.dot(left, mask.astype(jnp.float32), precision=lax.Precision.HIGHEST)
    return jnp.dot(middle, right, precision=lax.Precision.HIGHEST)


def contract_first(left, right):
    return lax.dot_general(
        left, right, (((0,), (0,)), ((), ())), preferred_element_type=jnp.float32
    )


def contract_last(left, right):
    return lax.dot_general(
        left, right, (((1,), (1,)), ((), ())), preferred_element_type=jnp.float32
    )


def per_device(
    tokens, gate_weight, up_weight, down_weight, gate_mask, up_mask, down_mask, out_grad
):
    row_index = lax.axis_index("row")
    col_index = lax.axis_index("col")
    feat_cols = gate_weight.shape[0]
    unit_cols = gate_weight.shape[1]
    keep_gate = expand_mask(
        gate_mask, col_index * feat_cols, feat_cols, row_index * unit_cols, unit_cols
    )
    keep_up = expand_mask(
        up_mask, col_index * feat_cols, feat_cols, row_index * unit_cols, unit_cols
    )
    keep_down = expand_mask(
        down_mask, row_index * unit_cols, unit_cols, col_index * feat_cols, feat_cols
    )
    zero = jnp.zeros((), jnp.bfloat16)
    kept_both = jnp.concatenate(
        [jnp.where(keep_gate > 0, gate_weight, zero), jnp.where(keep_up > 0, up_weight, zero)],
        axis=1,
    )
    kept_down = jnp.where(keep_down > 0, down_weight, zero)
    gathered = lax.all_gather(tokens, "row", axis=0, tiled=True)
    block = gathered
    both = lax.psum_scatter(
        jnp.dot(block, kept_both, preferred_element_type=jnp.float32),
        "col",
        scatter_dimension=0,
        tiled=True,
    )
    gate = both[:, :unit_cols]
    up_part = both[:, unit_cols:]
    sig = jax.nn.sigmoid(gate)
    hidden = (gate * sig * up_part).astype(jnp.bfloat16)
    hidden_all = lax.all_gather(hidden, "col", axis=0, tiled=True)
    block = hidden_all
    mixed = lax.psum_scatter(
        jnp.dot(block, kept_down, preferred_element_type=jnp.float32),
        "row",
        scatter_dimension=0,
        tiled=True,
    ).astype(jnp.bfloat16)
    grad_all = lax.all_gather(out_grad, "row", axis=0, tiled=True)
    down_grad = keep_down * contract_first(hidden_all, grad_all)
    block = grad_all
    hidden_grad = lax.psum_scatter(
        contract_last(block, kept_down), "col", scatter_dimension=0, tiled=True
    )
    dgate = hidden_grad * up_part * sig * (1.0 + gate * (1.0 - sig))
    dup = hidden_grad * gate * sig
    pre_grad = jnp.concatenate([dgate.astype(jnp.bfloat16), dup.astype(jnp.bfloat16)], axis=1)
    pre_all = lax.all_gather(pre_grad, "col", axis=0, tiled=True)
    weight_both = contract_first(gathered, pre_all)
    gate_grad = keep_gate * weight_both[:, :unit_cols]
    up_grad = keep_up * weight_both[:, unit_cols:]
    block = pre_all
    input_grad = lax.psum_scatter(
        contract_last(block, kept_both), "row", scatter_dimension=0, tiled=True
    ).astype(jnp.bfloat16)
    return (mixed, input_grad, gate_grad, up_grad, down_grad)


def solution(mesh):
    return jax.shard_map(
        per_device,
        mesh=mesh,
        in_specs=(
            P("row", "col"),
            P("col", "row"),
            P("col", "row"),
            P("row", "col"),
            P(),
            P(),
            P(),
            P("row", "col"),
        ),
        out_specs=(
            P("row", "col"),
            P("row", "col"),
            P("col", "row"),
            P("col", "row"),
            P("row", "col"),
        ),
        check_vma=False,
    )
```

profile of v0, /device:TPU:1, one launch (start us, length us, event | category | flops | bytes accessed | tf_op | source)
XLA Modules:
  0.0 784.6 jit_solution(13439907684614649693)
XLA Ops:
  7.2 0.7 all-gather.9.cloned.1.call-update
  7.9 0.7 all-gather.5.cloned.1.call-update
  8.7 1.0 fusion.5
  9.8 0.5 fusion.11
  10.3 78.1 %all-gather.9.cloned.1.call-done = bf16[2048,512]{1,0:T(8,128)(2,1)} async-done(((bf16[64,512]{1,0:T(8,128)(2,1)}), bf16[2048,512]{1,0:T(8,128)(2,1)}) %all-gather.9.cloned.1.call-update) | async-done | bytes 2097168 | tf_op jit(solution)/shard_map/all_gather | solution.py:74
  88.4 4.8 convolution_bitcast_fusion.1
  93.3 0.0 reduce-scatter.5.cloned.1.call-start
  93.3 0.6 copy-done.4
  94.0 0.3 fusion.1
  94.3 0.3 fusion.2
  94.6 1.4 compare_select_fusion.1
  96.0 1.4 compare_select_fusion.2
  97.4 68.7 %all-gather.5.cloned.1.call-done = bf16[2048,512]{1,0:T(8,128)(2,1)} async-done(((bf16[64,512]{1,0:T(8,128)(2,1)}), bf16[2048,512]{1,0:T(8,128)(2,1)}) %all-gather.5.cloned.1.call-update) | async-done | bytes 2097168 | tf_op jit(solution)/shard_map/all_gather | solution.py:54
  166.1 6.9 convolution_bitcast_fusion
  173.1 0.0 all-gather.7.cloned.1.call-start
  173.1 33.3 %reduce-scatter.9.cloned.1.call-done = f32[256,448]{0,1:T(8,128)} async-done(((f32[2048,448]{0,1:T(8,128)}), f32[256,448]{0,1:T(8,128)}) %reduce-scatter.9.cloned.1.call-update) | async-done | bytes 458768 | tf_op jit(solution)/shard_map/reduce_scatter | solution.py:77
  206.4 53.5 %reduce-scatter.5.cloned.1.call-done = f32[256,896]{0,1:T(8,128)} async-done(((f32[2048,896]{0,1:T(8,128)}), f32[256,896]{0,1:T(8,128)}) %reduce-scatter.5.cloned.1.call-update) | async-done | bytes 917520 | tf_op jit(solution)/shard_map/reduce_scatter | solution.py:56
  260.0 2.3 multiply_convert_fusion.1
  262.3 0.0 all-gather.11.cloned.1.call-start
  262.4 1.7 pad_maximum_fusion.3
  264.1 0.0 reduce-scatter.7.cloned.1.call-start
  264.2 27.6 %all-gather.7.cloned.1.call-done = bf16[2048,448]{0,1:T(8,128)(2,1)} async-done(((bf16[256,448]{0,1:T(8,128)(2,1)}), bf16[2048,448]{0,1:T(8,128)(2,1)}) %all-gather.7.cloned.1.call-update) | async-done | bytes 1835024 | tf_op jit(solution)/shard_map/all_gather | solution.py:66
  291.8 4.8 fusion.24
  296.6 34.9 %all-gather.11.cloned.1.call-done = bf16[2048,896]{0,1:T(8,128)(2,1)} async-done(((bf16[256,896]{0,1:T(8,128)(2,1)}), bf16[2048,896]{0,1:T(8,128)(2,1)}) %all-gather.11.cloned.1.call-update) | async-done | bytes 3670032 | tf_op jit(solution)/shard_map/all_gather | solution.py:83
  331.5 6.5 fusion
  338.1 4.3 convolution_multiply_fusion
  342.4 2.1 convolution_bitcast_fusion.2
  344.4 1.6 slice_multiply_fusion
  346.1 206.2 %reduce-scatter.7.cloned.1.call-done = f32[64,512]{1,0:T(8,128)} async-done(((f32[2048,512]{1,0:T(8,128)}), f32[64,512]{1,0:T(8,128)}) %reduce-scatter.7.cloned.1.call-update) | async-done | bytes 131088 | tf_op jit(solution)/shard_map/reduce_scatter | solution.py:68
  552.3 1.5 convert_element_type.34
  553.8 222.5 %reduce-scatter.11.cloned.1.call-done = f32[64,512]{1,0:T(8,128)} async-done(((f32[2048,512]{1,0:T(8,128)}), f32[64,512]{1,0:T(8,128)}) %reduce-scatter.11.cloned.1.call-update) | async-done | bytes 131088 | tf_op jit(solution)/shard_map/reduce_scatter | solution.py:88
  776.3 1.5 convert_element_type.37
  (27 shorter events, 0.3 us)
Async XLA Ops:
  7.2 81.2 %all-gather.9.cloned.1.call-start = ((), (), s32[]{:S(2)}) async-start(), calls=%async_computation.8 | async-start | bytes 2162688 | tf_op jit(solution)/shard_map/all_gather | solution.py:74
  7.9 158.2 %all-gather.5.cloned.1.call-start = ((), (), s32[]{:S(2)}) async-start(), calls=%async_computation.4 | async-start | bytes 2162688 | tf_op jit(solution)/shard_map/all_gather | solution.py:54
  8.7 197.8 %reduce-scatter.9.cloned.1.call-start = ((), (), s32[]{:S(2)}) async-start(), calls=%async_computation.9 | async-start | bytes 4128768 | tf_op jit(solution)/shard_map/reduce_scatter | solution.py:77
  93.2 0.7 copy-start.4
  93.2 1.0 copy-start.5
  93.2 1.4 copy-start.1
  93.3 2.8 copy-start.2
  93.3 166.7 %reduce-scatter.5.cloned.1.call-start = ((), (), s32[]{:S(2)}) async-start(), calls=%async_computation.5 | async-start | bytes 8257536 | tf_op jit(solution)/shard_map/reduce_scatter | solution.py:56
  173.1 118.7 %copy-start = (bf16[448,512]{1,0:T(8,128)(2,1)S(1)}, bf16[448,512]{1,0:T(8,128)(2,1)}, u32[]{:S(2)}) copy-start(bf16[448,512]{1,0:T(8,128)(2,1)} %param.11) | copy-start | bytes 1376260
  173.1 118.7 %all-gather.7.cloned.1.call-start = ((), (), s32[]{:S(2)}) async-start(), calls=%async_computation.6 | async-start | bytes 2064384 | tf_op jit(solution)/shard_map/all_gather | solution.py:66
  262.3 69.2 %all-gather.11.cloned.1.call-start = ((), (), s32[]{:S(2)}) async-start(), calls=%async_computation.10 | async-start | bytes 4128768 | tf_op jit(solution)/shard_map/all_gather | solution.py:83
  264.1 288.1 %reduce-scatter.7.cloned.1.call-start = ((), (), s32[]{:S(2)}) async-start(), calls=%async_computation.7 | async-start | bytes 4325376 | tf_op jit(solution)/shard_map/reduce_scatter | solution.py:68
  296.6 35.0 %copy-start.3 = (bf16[512,448]{0,1:T(8,128)(2,1)S(1)}, bf16[512,448]{0,1:T(8,128)(2,1)}, u32[]{:S(2)}) copy-start(bf16[512,448]{0,1:T(8,128)(2,1)} %get-tuple-element.10) | copy-start | bytes 1376260
  296.6 479.7 %reduce-scatter.11.cloned.1.call-start = ((), (), s32[]{:S(2)}) async-start(), calls=%async_computation.11 | async-start | bytes 4325376 | tf_op jit(solution)/shard_map/reduce_scatter | solution.py:88
  338.0 4.4 copy-start.6
  338.0 4.3 copy-start.7
Sparse Core Ops, SparseCore 0:
  10.6 77.7 all-gather.8
  91.0 75.1 all-gather.4
  168.7 37.6 reduce-scatter.8
  208.8 51.0 reduce-scatter.4
  262.4 29.3 all-gather.6
  294.0 37.4 all-gather.10
  335.4 216.8 reduce-scatter.6
  556.7 219.5 reduce-scatter.10
where the time goes:
time: 789 us; the launch traced here: 785 us
  waiting for transfers between devices  726 us (92%)
  matrix products  34.4 us (4%)
  between operations  14.2 us (2%)
  other arithmetic  8.8 us (1%)
    reduce_scatter x1, waiting for transfers between devices, per_device(): lax.psum_scatter(contract_last(block, kept_both), 'row', scatter_dimensio...  222 us
    reduce_scatter x1, waiting for transfers between devices, per_device(): lax.psum_scatter(jnp.dot(block, kept_down, preferred_element_type=jnp.flo...  206 us
    all_gather x1, waiting for transfers between devices, per_device(): grad_all = lax.all_gather(out_grad, 'row', axis=0, tiled=True)  78.1 us
    all_gather x1, waiting for transfers between devices, per_device(): gathered = lax.all_gather(tokens, 'row', axis=0, tiled=True)  68.7 us
    reduce_scatter x1, waiting for transfers between devices, per_device(): lax.psum_scatter(jnp.dot(block, kept_both, preferred_element_type=jnp.flo...  53.5 us
    all_gather x1, waiting for transfers between devices, per_device(): pre_all = lax.all_gather(pre_grad, 'col', axis=0, tiled=True)  34.9 us
    reduce_scatter x1, waiting for transfers between devices, per_device(): lax.psum_scatter(contract_last(block, kept_down), 'col', scatter_dimensio...  33.3 us
    all_gather x1, waiting for transfers between devices, per_device(): hidden_all = lax.all_gather(hidden, 'col', axis=0, tiled=True)  27.6 us
  transfers between devices with their start and end apart: 8, of which 8 were waited for; matrix products, arithmetic and copies ran while one was open for 5% of the time, Pallas kernels for 0%

commit v1 on v0

v1 whole, which is shorter than its diff:
```python
import functools

import jax
import jax.numpy as jnp
from jax import lax
from jax.experimental import pallas as pl
from jax.experimental.pallas import tpu as pltpu
from jax.sharding import PartitionSpec as P

BLOCK = 128
NX, NY, NZ = 4, 4, 8
T = 32
S = NX * T
FC = 512
F = 2 * FC
U = 448
DZ = (0, 1, -1, 2, -2, 3, -3, 4)
SLOT = {d % NZ: i for i, d in enumerate(DZ)}
GROUPS = ((0,), (1, 2), (3, 4), (5, 6), (7,))
BF = jnp.bfloat16
F32 = jnp.float32
MESH = pl.DeviceIdType.MESH


def nn(a, b):
    return jnp.dot(a, b, preferred_element_type=F32)


def nt(a, b):
    return lax.dot_general(a, b, (((1,), (1,)), ((), ())), preferred_element_type=F32)


def tn(a, b):
    return lax.dot_general(a, b, (((0,), (0,)), ((), ())), preferred_element_type=F32)


def kernel(
    tok, gw, uw, dw, gm, um, dm, og,
    mixed_o, ig_o, gg_o, ug_o, dg_o,
    ta, gb, to, go, gwo, uwo, dwo, wgu, kd, mg, mu, md,
    pf, pp, pr, hd, ho, mz, mr, mr0, p2, ir, si, iz, sm, mx,
    s_ax, s_bz, s_w, s_bx, s_az, s_ry, s_ay, s_ho, s_to, s_mz, s_mzh, s_ix, s_iz, s_mx,
    r_ax, r_bz, r_w, r_bx, r_az, r_ry, r_ay, r_ho, r_to, r_mz, r_ix, r_iz, r_mx,
):
    row, col = lax.axis_index("row"), lax.axis_index("col")
    z, x = row // NX, row % NX
    y, k = col // 2, col % 2

    def dev(dz, dx, dy, core):
        r = ((z + dz + NZ) % NZ) * NX + (x + dx) % NX
        return (r, ((y + dy) % NY) * 2 + core)

    sib = dev(0, 0, 0, 1 - k)

    def send(src, dst, ss, rs, to_dev):
        pltpu.make_async_remote_copy(
            src_ref=src, dst_ref=dst, send_sem=ss, recv_sem=rs, device_id=to_dev, device_id_type=MESH
        ).start()

    def local(src, dst, sem):
        pltpu.make_async_copy(src, dst, sem).start()

    def wait(ref, sem):
        pltpu.make_async_copy(ref, ref, sem).wait()

    def rows(start, size):
        return pl.ds(pl.multiple_of(start, 32), size)

    bar = pltpu.get_barrier_semaphore()
    partners = [sib]
    partners += [dev(0, e, 0, c) for e in range(1, NX) for c in (0, 1)]
    partners += [dev(e, 0, 0, c) for e in range(1, NZ) for c in (0, 1)]
    partners += [dev(0, 0, e, k) for e in range(1, NY)]
    for p in partners:
        pl.semaphore_signal(bar, inc=1, device_id=p, device_id_type=MESH)
    pl.semaphore_wait(bar, len(partners))

    mine = rows(x * T, T)
    for e in (1, 3, 2):
        for c in (0, 1):
            send(tok.at[pl.ds(c * T, T)], ta.at[k, mine], s_ax, r_ax, dev(0, e, 0, c))
    send(tok.at[rows((1 - k) * T, T)], ta.at[k, mine], s_ax, r_ax, sib)
    local(tok.at[rows(k * T, T)], ta.at[k, mine], r_ax)
    send(og.at[rows((1 - k) * T, T)], gb.at[k, mine], s_bz, r_bz.at[0], sib)
    local(og.at[rows(k * T, T)], gb.at[k, mine], r_bz.at[0])
    for d in DZ[1:]:
        s = SLOT[-d % NZ]
        for c in (0, 1):
            send(og.at[pl.ds(c * T, T)], gb.at[k, rows(s * S + x * T, T)], s_bz, r_bz.at[s], dev(d, 0, 0, c))
    send(gw, gwo, s_w.at[0], r_w.at[0], sib)
    send(uw, uwo, s_w.at[1], r_w.at[1], sib)
    send(dw, dwo, s_w.at[2], r_w.at[2], sib)

    def forward_tokens(s):
        d = DZ[s]
        if s == 0:
            wait(ta.at[:, pl.ds(0, S)], r_ax)
            steps = [(j, e) for j in (0, 1) for e in (1, -1)]
        else:
            e = -1 if d > 0 else 1
            js = ((0, 1) if abs(d) < 3 else ((0,) if d < 0 else (1,)))
            steps = [(j, e) for j in js]
        for j in (0, 1):
            if s:
                wait(ta.at[j, pl.ds(s * S, S)], r_az.at[s, j])
            for jj, e in steps:
                if jj == j:
                    t = SLOT[(d - e) % NZ]
                    send(ta.at[j, pl.ds(s * S, S)], ta.at[j, pl.ds(t * S, S)], s_az.at[j], r_az.at[t, j], dev(e, 0, 0, k))

    def last_tokens():
        for j in (0, 1):
            wait(ta.at[j, pl.ds(7 * S, S)], r_az.at[7, j])

    def forward_grads(s):
        mine = rows(s * S + x * T, T)
        wait(gb.at[:, pl.ds(s * S, T)], r_bz.at[s])
        for e in (1, 3, 2):
            send(gb.at[:, mine], gb.at[:, mine], s_bx.at[e - 1], r_bx.at[s], dev(0, e, 0, k))

    def unit_block(shape, dim):
        return (row * U + lax.broadcasted_iota(jnp.int32, shape, dim)) // BLOCK

    def masks():
        cols = (unit_block((112, U), 1) == lax.broadcasted_iota(jnp.int32, (112, U), 0)).astype(F32)
        mg[...] = nn(gm[pl.ds(pl.multiple_of(8 * y, 8), 8), :].astype(F32), cols)
        mu[...] = nn(um[pl.ds(pl.multiple_of(8 * y, 8), 8), :].astype(F32), cols)
        left = (unit_block((U, 112), 0) == lax.broadcasted_iota(jnp.int32, (U, 112), 1)).astype(F32)
        feat = (y * F + lax.broadcasted_iota(jnp.int32, (32, F), 1)) // BLOCK
        right = (feat == lax.broadcasted_iota(jnp.int32, (32, F), 0)).astype(F32)
        md[...] = nn(nn(left, dm[...].astype(F32)), right).astype(BF)

    zero = jnp.zeros((), BF)

    def keep_weights(core, g_ref, u_ref, d_ref):
        for b in range(FC // BLOCK):
            r = pl.ds(pl.multiple_of(core * FC + b * BLOCK, BLOCK), BLOCK)
            blk = pl.ds(b * BLOCK, BLOCK)
            m = pl.ds(core * (FC // BLOCK) + b, 1)
            g = jnp.where(jnp.broadcast_to(mg[m, :], (BLOCK, U)) > 0, g_ref[blk, :].astype(F32), 0.0)
            u = jnp.where(jnp.broadcast_to(mu[m, :], (BLOCK, U)) > 0, u_ref[blk, :].astype(F32), 0.0)
            wgu[r, :] = jnp.concatenate([g, u], axis=1).astype(BF)
        c = pl.ds(pl.multiple_of(core * FC, FC), FC)
        kd[:, c] = (md[:, c].astype(F32) * d_ref[...].astype(F32)).astype(BF)

    def stage1(s):
        wait(gb.at[:, pl.ds(0, 3 * T)], r_bx.at[s])
        r = pl.ds(s * S, S)
        both = nn(ta[0, r, :], wgu[0:FC, :]) + nn(ta[1, r, :], wgu[FC:F, :])
        back = nt(gb[0, r, :], kd[:, 0:FC]) + nt(gb[1, r, :], kd[:, FC:F])
        pf[r, 0 : 2 * U] = both
        pf[r, 2 * U : 3 * U] = back
        pp[r, 0 : 2 * U] = both.astype(BF)
        pp[r, 2 * U : 3 * U] = back.astype(BF)
        for e in (1, 3, 2):
            other = (y + e) % NY
            send(pp.at[rows(s * S + other * T, T)], pr.at[e - 1, pl.ds(s * T, T)], s_ry.at[e - 1], r_ry.at[s], dev(0, 0, e, k))

    def elementwise(s):
        wait(pp.at[pl.ds(0, 3 * T)], r_ry.at[s])
        mine = rows(s * S + y * T, T)
        r = pl.ds(s * T, T)
        tot = (pf[mine, :] + pr[0, r, :].astype(F32)) + (pr[1, r, :].astype(F32) + pr[2, r, :].astype(F32))
        gate, up, hg = tot[:, 0:U], tot[:, U : 2 * U], tot[:, 2 * U : 3 * U]
        sig = 1.0 / (1.0 + jnp.exp(-gate))
        act = gate * sig
        dgate = hg * up * sig * (1.0 + gate * (1.0 - sig))
        dup = hg * act
        hd[mine, :] = jnp.concatenate([dgate, dup, act * up], axis=1).astype(BF)

    def share(s):
        mine = rows(s * S + y * T, T)
        for e in (1, 3, 2):
            send(hd.at[mine], hd.at[mine], s_ay.at[e - 1], r_ay.at[s], dev(0, 0, e, k))

    def stage2(s):
        d = DZ[s]
        r = pl.ds(s * S, S)
        wait(hd.at[pl.ds(0, 3 * T)], r_ay.at[s])
        send(hd.at[r], ho.at[r], s_ho, r_ho, sib)
        part = nn(hd[r, 2 * U : 3 * U], kd[...])
        if s == 7:
            mz[r, :] = part.astype(BF)
            send(mz.at[r, 0:FC], mr.at[pl.ds(6 * S, S), 0:FC], s_mzh.at[0], r_mz.at[6], dev(-1, 0, 0, k))
            send(mz.at[r, FC:F], mr.at[pl.ds(5 * S, S), FC:F], s_mzh.at[1], r_mz.at[5], dev(1, 0, 0, k))
        elif abs(d) == 3:
            half = slice(0, FC) if d < 0 else slice(FC, F)
            rest = slice(FC, F) if d < 0 else slice(0, FC)
            mz[r, rest] = part[:, rest].astype(BF)
            wait(mr.at[r, half], r_mz.at[s])
            mz[r, half] = (part[:, half] + mr[r, half].astype(F32)).astype(BF)
            t = 4 if d < 0 else 3
            send(mz.at[r], mr.at[pl.ds(t * S, S)], s_mz.at[0 if d < 0 else 1], r_mz.at[t], dev(-1 if d < 0 else 1, 0, 0, k))
        elif s:
            wait(mr.at[r], r_mz.at[s])
            mz[r, :] = (part + mr[r, :].astype(F32)).astype(BF)
            down = d < 0
            if abs(d) == 2:
                t = 2 if down else 1
                send(mz.at[r], mr.at[pl.ds(t * S, S)], s_mz.at[0 if down else 1], r_mz.at[t], dev(-1 if down else 1, 0, 0, k))
            else:
                send(mz.at[r], mr0.at[0 if down else 1], s_mz.at[0 if down else 1], r_mz.at[0 if down else 7], dev(-1 if down else 1, 0, 0, k))
        else:
            wait(mr0.at[0], r_mz.at[0])
            wait(mr0.at[1], r_mz.at[7])
            sm[...] = part + (mr0[0].astype(F32) + mr0[1].astype(F32))
            for e in (1, 3, 2):
                other = (x + e) % NX
                for c in (0, 1):
                    send(sm.at[rows(other * T, T), c * FC : (c + 1) * FC], mx.at[k, mine], s_mx, r_mx, dev(0, e, 0, c))
            for c in (0, 1):

                @pl.when(k == c)
                def _():
                    send(sm.at[mine, (1 - c) * FC : (2 - c) * FC], mx.at[c, mine], s_mx, r_mx, sib)
                    local(sm.at[mine, c * FC : (c + 1) * FC], mx.at[c, mine], r_mx)

    def stage2_inputs(s):
        r = pl.ds(s * S, S)
        p2[r, :] = nt(hd[r, 0 : 2 * U], wgu[...]).astype(BF)
        for e in (1, 3, 2):
            other = (x + e) % NX
            send(p2.at[rows(s * S + other * T, T)], ir.at[e - 1, pl.ds(s * T, T)], s_ix.at[e - 1], r_ix.at[s], dev(0, e, 0, k))

    def reduce_inputs(s):
        d = DZ[s]
        wait(p2.at[pl.ds(0, 3 * T)], r_ix.at[s])
        r = pl.ds(s * T, T)
        own = p2[rows(s * S + x * T, T), :].astype(F32)
        si[r, :] = ((own + ir[0, r, :].astype(F32)) + (ir[1, r, :].astype(F32) + ir[2, r, :].astype(F32))).astype(BF)
        t = SLOT[-d % NZ]
        if s:
            for c in (0, 1):
                send(si.at[r, c * FC : (c + 1) * FC], iz.at[k, pl.ds(t * T, T)], s_iz, r_iz, dev(d, 0, 0, c))
        else:
            for c in (0, 1):

                @pl.when(k == c)
                def _():
                    send(si.at[r, (1 - c) * FC : (2 - c) * FC], iz.at[c, r], s_iz, r_iz, sib)
                    local(si.at[r, c * FC : (c + 1) * FC], iz.at[c, r], r_iz)

    masks()
    keep_weights(k, gw, uw, dw)
    forward_tokens(0)
    forward_grads(0)
    for s in GROUPS[1]:
        forward_grads(s)
    wait(gwo, r_w.at[0])
    wait(uwo, r_w.at[1])
    wait(dwo, r_w.at[2])
    keep_weights(1 - k, gwo, uwo, dwo)
    stage1(0)
    for s in GROUPS[1]:
        forward_tokens(s)
    for s in GROUPS[2]:
        forward_grads(s)
    for s in GROUPS[1]:
        stage1(s)
    elementwise(0)
    for s in GROUPS[2]:
        forward_tokens(s)
    for s in GROUPS[3] + GROUPS[4]:
        forward_grads(s)
    for s in GROUPS[2]:
        stage1(s)
    for s in GROUPS[1]:
        elementwise(s)
    for s in GROUPS[3]:
        forward_tokens(s)
    for s in GROUPS[3]:
        stage1(s)
    for s in GROUPS[2]:
        elementwise(s)
    last_tokens()
    stage1(7)
    for s in GROUPS[3]:
        elementwise(s)
    elementwise(7)
    share(7)
    for s in GROUPS[3]:
        share(s)
    send(ta.at[1 - k], to, s_to.at[0], r_to.at[0], sib)
    send(gb.at[1 - k], go, s_to.at[1], r_to.at[1], sib)
    for s in GROUPS[2]:
        share(s)
    for i in (4, 3, 2, 1, 0):
        for s in GROUPS[i]:
            stage2(s)
        if i >= 2:
            for s in GROUPS[i - 2]:
                share(s) if i - 2 < 2 else None
        for s in GROUPS[i]:
            stage2_inputs(s)
        if i < 4:
            for s in GROUPS[i + 1]:
                reduce_inputs(s)
    reduce_inputs(0)

    wait(to, r_to.at[0])
    wait(go, r_to.at[1])
    wait(ho, r_ho)
    for b in range(FC // BLOCK):
        c = pl.ds(b * BLOCK, BLOCK)
        grad = tn(ta[k, :, c], hd[:, 0 : 2 * U]) + tn(to[:, c], ho[:, 0 : 2 * U])
        m = pl.ds(k * (FC // BLOCK) + b, 1)
        gg_o[c, :] = jnp.where(jnp.broadcast_to(mg[m, :], (BLOCK, U)) > 0, grad[:, 0:U], 0.0)
        ug_o[c, :] = jnp.where(jnp.broadcast_to(mu[m, :], (BLOCK, U)) > 0, grad[:, U : 2 * U], 0.0)
    grad = tn(hd[:, 2 * U : 3 * U], gb[k]) + tn(ho[:, 2 * U : 3 * U], go[...])
    dg_o[...] = grad * md[:, pl.ds(pl.multiple_of(k * FC, FC), FC)].astype(F32)

    wait(mx, r_mx)
    for c in (0, 1):
        part = [mx[c, i * T : (i + 1) * T, :] for i in range(NX)]
        mixed_o[c * T : (c + 1) * T, :] = ((part[0] + part[1]) + (part[2] + part[3])).astype(BF)
    wait(iz, r_iz)
    for c in (0, 1):
        part = [iz[c, i * T : (i + 1) * T, :].astype(F32) for i in range(NZ)]
        low = (part[0] + part[1]) + (part[2] + part[3])
        high = (part[4] + part[5]) + (part[6] + part[7])
        ig_o[c * T : (c + 1) * T, :] = (low + high).astype(BF)

    wait(ta.at[0, pl.ds(0, 7 * T)], s_ax)
    wait(gb.at[0, pl.ds(0, 15 * T)], s_bz)
    wait(gwo, s_w.at[0])
    wait(uwo, s_w.at[1])
    wait(dwo, s_w.at[2])
    for e in range(3):
        wait(gb.at[:, pl.ds(0, 8 * T)], s_bx.at[e])
        wait(pp.at[pl.ds(0, 8 * T)], s_ry.at[e])
        wait(hd.at[pl.ds(0, 8 * T)], s_ay.at[e])
        wait(p2.at[pl.ds(0, 8 * T)], s_ix.at[e])
    for j in (0, 1):
        wait(ta.at[j, pl.ds(0, 7 * S)], s_az.at[j])
        wait(to, s_to.at[j])
        wait(mz.at[pl.ds(0, 3 * S)], s_mz.at[j])
        wait(mz.at[pl.ds(0, S), 0:FC], s_mzh.at[j])
    wait(ho, s_ho)
    wait(gb.at[0, pl.ds(0, 15 * T)], s_iz)
    wait(ta.at[:, pl.ds(0, 7 * T)], s_mx)


def per_device(tokens, gate_weight, up_weight, down_weight, gate_mask, up_mask, down_mask, out_grad):
    vmem = pl.BlockSpec(memory_space=pltpu.VMEM)
    dma = pltpu.SemaphoreType.DMA
    v = pltpu.VMEM
    return pl.pallas_call(
        kernel,
        out_shape=(
            jax.ShapeDtypeStruct((2 * T, FC), BF),
            jax.ShapeDtypeStruct((2 * T, FC), BF),
            jax.ShapeDtypeStruct((FC, U), F32),
            jax.ShapeDtypeStruct((FC, U), F32),
            jax.ShapeDtypeStruct((U, FC), F32),
        ),
        in_specs=[vmem] * 8,
        out_specs=(vmem,) * 5,
        scratch_shapes=[
            v((2, NZ * S, FC), BF),
            v((2, NZ * S, FC), BF),
            v((NZ * S, FC), BF),
            v((NZ * S, FC), BF),
            v((FC, U), BF),
            v((FC, U), BF),
            v((U, FC), BF),
            v((F, 2 * U), BF),
            v((U, F), BF),
            v((8, U), F32),
            v((8, U), F32),
            v((U, F), BF),
            v((NZ * S, 3 * U), F32),
            v((NZ * S, 3 * U), BF),
            v((3, NZ * T, 3 * U), BF),
            v((NZ * S, 3 * U), BF),
            v((NZ * S, 3 * U), BF),
            v((NZ * S, F), BF),
            v((NZ * S, F), BF),
            v((2, S, F), BF),
            v((NZ * S, F), BF),
            v((3, NZ * T, F), BF),
            v((NZ * T, F), BF),
            v((2, NZ * T, FC), BF),
            v((S, F), F32),
            v((2, S, FC), F32),
            dma, dma, dma((3,)), dma((3,)), dma((2,)), dma((3,)), dma((3,)), dma, dma((2,)), dma((2,)), dma((2,)), dma((3,)), dma, dma,
            dma, dma((8,)), dma((3,)), dma((8,)), dma((8, 2)), dma((8,)), dma((8,)), dma, dma((2,)), dma((8,)), dma((8,)), dma, dma,
        ],
        compiler_params=pltpu.CompilerParams(
            collective_id=0, has_side_effects=True, vmem_limit_bytes=60 << 20
        ),
        cost_estimate=pl.CostEstimate(flops=9_000_000_000, bytes_accessed=8 << 20, transcendentals=120_000),
        name="sublayer",
    )(tokens, gate_weight, up_weight, down_weight, gate_mask, up_mask, down_mask, out_grad)


def solution(mesh):
    return jax.shard_map(
        per_device,
        mesh=mesh,
        in_specs=(
            P("row", "col"), P("col", "row"), P("col", "row"), P("row", "col"), P(), P(), P(), P("row", "col"),
        ),
        out_specs=(P("row", "col"), P("row", "col"), P("col", "row"), P("col", "row"), P("row", "col")),
        check_vma=False,
    )
```

time: 789 us -> 127 us (0.16)
  waiting for transfers between devices: 726 us -> 0 us
  Pallas kernels: 0 us -> 115 us
  matrix products: 34.4 us -> 0 us
  between operations: 14.2 us -> 0.66 us
  local copies, waits for them, and re-layouts: 0.66 us -> 10.7 us
  other arithmetic: 8.8 us -> 0 us
    reduce_scatter x4 -> x0, waiting for transfers between devices: 515 us -> none  [the longest x1 222 us: per_device(): lax.psum_scatter(contract_last(block, kept_both), 'row', scatter_dimensio...]
    all_gather x4 -> x0, waiting for transfers between devices: 209 us -> none  [the longest x1 78.1 us: per_device(): grad_all = lax.all_gather(out_grad, 'row', axis=0, tiled=True)]
    pallas_call x0 -> x1, Pallas kernels: none -> 115 us  [per_device(): pl.pallas_call(kernel, out_shape=(jax.ShapeDtypeStruct((2 * T, FC), BF),...]
    dot_general x12 -> x0, matrix products: 34.4 us -> none  [the longest x2 11.3 us: contract_last(): lax.dot_general(left, right, (((1,), (1,)), ((), ())), preferred_element_...]
  transfers between devices with their start and end apart: 8 -> 0, of which waited for: 8 -> 0; matrix products, arithmetic and copies ran while one was open for 5% -> 0% of each run, Pallas kernels for 0% -> 0%
where the time goes in v1:
time: 127 us; the launch traced here: 126 us
  Pallas kernels  115 us (91%)
  local copies, waits for them, and re-layouts  10.7 us (8%)
    pallas_call x1, Pallas kernels, per_device(): pl.pallas_call(kernel, out_shape=(jax.ShapeDtypeStruct((2 * T, FC), BF),...  115 us
    unnamed x16, local copies, waits for them, and re-layouts  6.94 us
    pallas_call x2, local copies, waits for them, and re-layouts, per_device(): pl.pallas_call(kernel, out_shape=(jax.ShapeDtypeStruct((2 * T, FC), BF),...  3.8 us

profile of v1, /device:TPU:1, one launch (start us, length us, event | category | flops | bytes accessed | tf_op | source)
XLA Modules:
  0.0 126.2 jit_solution(18249813599959376535)
XLA Ops:
  0.6 1.4 %copy.15.dm = s32[112,32]{1,0:T(8,128)} copy(s32[112,32]{0,1:T(8,128)} %param.14) | data formatting | bytes 28672 | tf_op args[6]
  2.1 0.0 copy-start.2
  2.1 2.1 %copy.13.gw = bf16[512,448]{1,0:T(8,128)(2,1)} copy(bf16[512,448]{0,1:T(8,128)(2,1)} %param.9) | data formatting | bytes 917504 | tf_op args[1]
  4.1 0.0 copy-done.2
  4.1 1.0 copy.14.uw
  5.1 114.8 %sublayer.1 = (bf16[64,512]{1,0:T(8,128)(2,1)}, bf16[64,512]{1,0:T(8,128)(2,1)}, f32[512,448]{1,0:T(8,128)}, f32[512,448]{1,0:T(8,128)}, f32[448,512]{1,0:T(8,128)}) custom-call(bf16[64,512]{1,0:T(8,128)(2,1)} %tok.1, bf16[512,448]{1,0:T(8,128)(2,1)} %copy.13.gw, bf16[512,448]{1,0:T(8,128)(2,1)} %copy.14.uw, bf16[448,512]{1,0:T(8,128)(2,1)} %dw.1, ...), custom_call_target="tpu_custom_call" | custom-call | flops 8999999488 | bytes 8388608 | tf_op jit(solution)/shard_map/sublayer/pallas_call | solution.py:347
  120.0 0.0 copy-start
  120.0 2.6 %copy.16 = f32[512,448]{0,1:T(8,128)} copy(f32[512,448]{1,0:T(8,128)} %get-tuple-element.7) | data formatting | bytes 1835008 | tf_op jit(solution)/shard_map/sublayer/pallas_call | solution.py:347
  122.5 0.0 copy-done
  122.5 0.0 copy-start.4
  122.6 0.0 copy-start.1
  122.6 1.2 copy.17
  123.8 0.0 copy-done.4
  123.8 0.0 copy-start.3
  123.8 0.6 copy.21
  124.4 0.2 copy-done.3
  124.7 0.6 copy.22
  125.3 0.0 copy-done.1
  125.3 0.9 copy.23
Async XLA Ops:
  2.1 2.1 %copy-start.2 = (bf16[512,448]{0,1:T(8,128)(2,1)S(1)}, bf16[512,448]{0,1:T(8,128)(2,1)}, u32[]{:S(2)}) copy-start(bf16[512,448]{0,1:T(8,128)(2,1)} %param.10) | copy-start | bytes 1376260
  120.0 2.6 %copy-start = (f32[512,448]{1,0:T(8,128)S(1)}, f32[512,448]{1,0:T(8,128)}, u32[]{:S(2)}) copy-start(f32[512,448]{1,0:T(8,128)} %get-tuple-element.8) | copy-start | bytes 2752516
  122.5 1.2 copy-start.4
  122.6 2.7 %copy-start.1 = (f32[448,512]{1,0:T(8,128)S(1)}, f32[448,512]{1,0:T(8,128)}, u32[]{:S(2)}) copy-start(f32[448,512]{1,0:T(8,128)} %get-tuple-element.19) | copy-start | bytes 2752516
  123.8 0.9 copy-start.3

commit v2 on v0

v2 whole, which is shorter than its diff:
```python
import functools

import jax
import jax.numpy as jnp
from jax import lax
from jax.experimental import pallas as pl
from jax.experimental.pallas import tpu as pltpu
from jax.sharding import PartitionSpec as P

BLOCK = 128
NX, NY, NZ = 4, 4, 8
H = 32
NC = 2
T = H // NC
S = NX * T
NS = NC * NZ
FC = 512
F = 2 * FC
U = 448
UP = 512
W = 2 * U + UP
DZ = (0, 1, -1, 2, -2, 3, -3, 4)
SLOT = {d % NZ: i for i, d in enumerate(DZ)}
GROUPS = ((0,), (1, 2), (3, 4), (5, 6), (7,))
ORDER = (
    "A0 G0 A1 W",
    "B00 G1 M B01",
    "F00 N B02 P00",
    "F01 B03 P01 F02",
    "P02 B04 F10 B10",
    "F03 P03 B11 F04",
    "P04 E02 E01 B12",
    "F11 S02 E04 S04",
    "E03 F12 S03 B13",
    "E00 P12 F13 Q04",
    "Q03 S01 B14 P11",
    "Q02 Z04 F14 P14",
    "Z03 P13 I03 E12",
    "I04 E14 S14 S00",
    "Z02 I02 E13 S13",
    "Q01 E11 Z01 Q14",
    "I01 S12 I14 P10",
    "Q00 Z14 I00 Q13",
    "Z13 I13 R02 S11",
    "Z00 Q12 Z12 E10",
    "R01 I12 S10 X",
    "R04 Q11 I11 Z11",
    "Q10 R14 R13 I10",
    "R00 Z10 R03 R12",
    "R10 R11",
)
BF = jnp.bfloat16
F32 = jnp.float32
MESH = pl.DeviceIdType.MESH


def nn(a, b):
    return jnp.dot(a, b, preferred_element_type=F32)


def nt(a, b):
    return lax.dot_general(a, b, (((1,), (1,)), ((), ())), preferred_element_type=F32)


def tn(a, b):
    return lax.dot_general(a, b, (((0,), (0,)), ((), ())), preferred_element_type=F32)


def kernel(
    tok, gw, uw, dw, gm, um, dm, og,
    mixed_o, ig_o, gg_o, ug_o, dg_o,
    ta, gb, to, go, gwo, uwo, dwo, wgu, kd, keep,
    pf, pp, pr, hd, ho, mp, mz, mr, mr0, p2, ir, si, iz, sm, mx,
    s_ax, s_bz, s_w, s_bx, s_bh, s_az, s_ry, s_ay, s_ho, s_to, s_mz, s_mzh, s_ix, s_iz, s_mx,
    r_ax, r_bz, r_w, r_bx, r_az, r_ry, r_ay, r_ho, r_to, r_mz, r_ix, r_iz, r_mx,
):
    row, col = lax.axis_index("row"), lax.axis_index("col")
    z, x = row // NX, row % NX
    y, k = col // 2, col % 2

    def dev(dz, dx, dy, core):
        r = ((z + dz + NZ) % NZ) * NX + (x + dx) % NX
        return (r, ((y + dy) % NY) * 2 + core)

    sib = dev(0, 0, 0, 1 - k)

    def send(src, dst, ss, rs, to_dev):
        pltpu.make_async_remote_copy(
            src_ref=src, dst_ref=dst, send_sem=ss, recv_sem=rs, device_id=to_dev, device_id_type=MESH
        ).start()

    def local(src, dst, sem):
        pltpu.make_async_copy(src, dst, sem).start()

    def wait(ref, sem):
        pltpu.make_async_copy(ref, ref, sem).wait()

    def rows(start, size):
        return pl.ds(pl.multiple_of(start, 16), size)

    bar = pltpu.get_barrier_semaphore()
    partners = [sib]
    partners += [dev(0, e, 0, c) for e in range(1, NX) for c in (0, 1)]
    partners += [dev(e, 0, 0, c) for e in range(1, NZ) for c in (0, 1)]
    partners += [dev(0, 0, e, k) for e in range(1, NY)]
    for p in partners:
        pl.semaphore_signal(bar, inc=1, device_id=p, device_id_type=MESH)
    pl.semaphore_wait(bar, len(partners))

    def part_of(core, c):
        return rows(core * H + c * T, T)

    def block(c, s):
        return rows((c * NZ + s) * S + x * T, T)

    def start_tokens(c):
        mine = block(c, 0)
        for e in (1, 3, 2):
            for core in (0, 1):
                send(tok.at[part_of(core, c)], ta.at[k, mine], s_ax, r_ax.at[c], dev(0, e, 0, core))
        send(tok.at[part_of(1 - k, c)], ta.at[k, mine], s_ax, r_ax.at[c], sib)
        local(tok.at[part_of(k, c)], ta.at[k, mine], r_ax.at[c])

    def start_grads(c):
        send(og.at[part_of(1 - k, c)], gb.at[k, block(c, 0)], s_bz, r_bz.at[c, 0], sib)
        local(og.at[part_of(k, c)], gb.at[k, block(c, 0)], r_bz.at[c, 0])
        for e in (1, -1):
            t = SLOT[-e % NZ]
            for core in (0, 1):
                send(og.at[part_of(core, c)], gb.at[k, block(c, t)], s_bz, r_bz.at[c, t], dev(e, 0, 0, core))

    def forward_tokens(c, s):
        d = DZ[s]
        r = pl.ds((c * NZ + s) * S, S)
        if s == 0:
            wait(ta.at[:, r], r_ax.at[c])
        for j in (0, 1):
            if s:
                wait(ta.at[j, r], r_az.at[c, s, j])
            ahead = (1, -1) if s == 0 else (-1 if d > 0 else 1,)
            if s == 7 or (abs(d) == 3 and (d < 0) != (j == 1)):
                ahead = ()
            for e in ahead:
                t = SLOT[(d - e) % NZ]
                send(ta.at[j, r], ta.at[j, pl.ds((c * NZ + t) * S, S)], s_az.at[j], r_az.at[c, t, j], dev(e, 0, 0, k))

    def forward_grads(c, s):
        d = DZ[s]
        mine = block(c, s)
        wait(gb.at[:, pl.ds(0, T)], r_bz.at[c, s])
        e = -1 if d > 0 else 1
        if 0 < abs(d) < 4:
            t = SLOT[(d - e) % NZ]
            there = block(c, t)
            if abs(d) < 3:
                send(gb.at[:, mine], gb.at[:, there], s_bh.at[0], r_bz.at[c, t], dev(e, 0, 0, k))
            else:
                j = 0 if d < 0 else 1
                send(gb.at[j, mine], gb.at[j, there], s_bh.at[1], r_bz.at[c, t], dev(e, 0, 0, k))
        for e in (1, 3, 2):
            send(gb.at[:, mine], gb.at[:, mine], s_bx.at[e - 1], r_bx.at[c, s], dev(0, e, 0, k))

    def start_weights():
        send(gw, gwo, s_w.at[0], r_w.at[0], sib)
        send(uw, uwo, s_w.at[1], r_w.at[1], sib)
        send(dw, dwo, s_w.at[2], r_w.at[2], sib)

    def masks():
        unit = (row * U + lax.broadcasted_iota(jnp.int32, (U, 112), 0)) // BLOCK
        left = (unit == lax.broadcasted_iota(jnp.int32, (U, 112), 1)).astype(F32)
        feat = (y * F + lax.broadcasted_iota(jnp.int32, (32, F), 1)) // BLOCK
        right = (feat == lax.broadcasted_iota(jnp.int32, (32, F), 0)).astype(F32)
        for i, ref in enumerate((gm, um, dm)):
            keep[i] = nn(nt(left, ref[...].astype(F32)), right).astype(BF)

    def keep_weights(core, g_ref, u_ref, d_ref):
        c = pl.ds(pl.multiple_of(core * FC, FC), FC)
        wgu[0:U, c] = keep[0, :, c] * g_ref[...]
        wgu[U : 2 * U, c] = keep[1, :, c] * u_ref[...]
        kd[0:U, c] = keep[2, :, c] * d_ref[...]
        kd[U:UP, c] = jnp.zeros((UP - U, FC), BF)

    def stage1(c, slots):
        r = pl.ds((c * NZ + slots[0]) * S, len(slots) * S)
        for s in slots:
            wait(gb.at[:, pl.ds(0, 3 * T)], r_bx.at[c, s])
        both = nt(ta[0, r, :], wgu[:, 0:FC]) + nt(ta[1, r, :], wgu[:, FC:F])
        back = nt(gb[0, r, :], kd[:, 0:FC]) + nt(gb[1, r, :], kd[:, FC:F])
        pf[r, 0 : 2 * U] = both
        pf[r, 2 * U : W] = back
        pp[r, 0 : 2 * U] = both.astype(BF)
        pp[r, 2 * U : W] = back.astype(BF)
        for s in slots:
            g = c * NZ + s
            for e in (1, 3, 2):
                other = (y + e) % NY
                send(pp.at[rows(g * S + other * T, T)], pr.at[e - 1, pl.ds(g * T, T)], s_ry.at[e - 1], r_ry.at[c, s], dev(0, 0, e, k))

    def elementwise(c, s):
        g = c * NZ + s
        wait(pp.at[pl.ds(0, 3 * T)], r_ry.at[c, s])
        mine = rows(g * S + y * T, T)
        r = pl.ds(g * T, T)
        tot = (pf[mine, :] + pr[0, r, :].astype(F32)) + (pr[1, r, :].astype(F32) + pr[2, r, :].astype(F32))
        gate, up, hg = tot[:, 0:U], tot[:, U : 2 * U], tot[:, 2 * U : 3 * U]
        sig = 1.0 / (1.0 + jnp.exp(-gate))
        act = gate * sig
        dgate = hg * up * sig * (1.0 + gate * (1.0 - sig))
        dup = hg * act
        hd[mine, :] = jnp.concatenate([dgate, dup, act * up, jnp.zeros((T, UP - U), F32)], axis=1).astype(BF)

    def share(c, s):
        g = c * NZ + s
        mine = rows(g * S + y * T, T)
        for e in (1, 3, 2):
            send(hd.at[mine], hd.at[mine], s_ay.at[e - 1], r_ay.at[c, s], dev(0, 0, e, k))

    def stage2(c, slots):
        r = pl.ds((c * NZ + slots[0]) * S, len(slots) * S)
        for s in slots:
            wait(hd.at[pl.ds(0, 3 * T)], r_ay.at[c, s])
        mp[r, :] = nn(hd[r, 2 * U : W], kd[...])
        p2[r, :] = nn(hd[r, 0 : 2 * U], wgu[...]).astype(BF)
        send(hd.at[r], ho.at[r], s_ho, r_ho, sib)

    def send_inputs(c, s):
        g = c * NZ + s
        for e in (1, 3, 2):
            other = (x + e) % NX
            send(p2.at[rows(g * S + other * T, T)], ir.at[e - 1, pl.ds(g * T, T)], s_ix.at[e - 1], r_ix.at[c, s], dev(0, e, 0, k))

    def pass_mixed(c, s):
        d = DZ[s]
        r = pl.ds((c * NZ + s) * S, S)
        way = 0 if d < 0 else 1
        ahead = dev(-1 if d < 0 else 1, 0, 0, k)
        if s == 7:
            mz[r, :] = mp[r, :].astype(BF)
            for way, t in ((0, 6), (1, 5)):
                half = slice(way * FC, (way + 1) * FC)
                there = pl.ds((c * NZ + t) * S, S)
                send(mz.at[r, half], mr.at[there, half], s_mzh.at[way], r_mz.at[c, t], dev(2 * way - 1, 0, 0, k))
        elif s:
            if abs(d) == 3:
                half = slice(way * FC, (way + 1) * FC)
                rest = slice((1 - way) * FC, (2 - way) * FC)
                mz[r, rest] = mp[r, rest].astype(BF)
                wait(mr.at[r, half], r_mz.at[c, s])
                mz[r, half] = (mp[r, half] + mr[r, half].astype(F32)).astype(BF)
            else:
                wait(mr.at[r], r_mz.at[c, s])
                mz[r, :] = (mp[r, :] + mr[r, :].astype(F32)).astype(BF)
            if abs(d) == 1:
                send(mz.at[r], mr0.at[c, way], s_mz.at[way], r_mz.at[c, 7 * way], ahead)
            else:
                t = s - 2
                send(mz.at[r], mr.at[pl.ds((c * NZ + t) * S, S)], s_mz.at[way], r_mz.at[c, t], ahead)
        else:
            wait(mr0.at[c, 0], r_mz.at[c, 0])
            wait(mr0.at[c, 1], r_mz.at[c, 7])
            tot = mp[r, :] + (mr0[c, 0].astype(F32) + mr0[c, 1].astype(F32))
            sm[c, 0] = tot[:, 0:FC]
            sm[c, 1] = tot[:, FC:F]
            mine = rows(x * T, T)
            for e in (1, 3, 2):
                other = rows((x + e) % NX * T, T)
                for core in (0, 1):
                    send(sm.at[c, core, other], mx.at[c, k, mine], s_mx, r_mx.at[c], dev(0, e, 0, core))
            send(sm.at[c, 1 - k, mine], mx.at[c, k, mine], s_mx, r_mx.at[c], sib)
            local(sm.at[c, k, mine], mx.at[c, k, mine], r_mx.at[c])

    def reduce_inputs(c, s):
        d = DZ[s]
        g = c * NZ + s
        wait(p2.at[pl.ds(0, 3 * T)], r_ix.at[c, s])
        r = pl.ds(g * T, T)
        own = p2[rows(g * S + x * T, T), :].astype(F32)
        tot = ((own + ir[0, r, :].astype(F32)) + (ir[1, r, :].astype(F32) + ir[2, r, :].astype(F32))).astype(BF)
        si[0, r, :] = tot[:, 0:FC]
        si[1, r, :] = tot[:, FC:F]
        t = pl.ds((c * NZ + SLOT[-d % NZ]) * T, T)
        if s:
            for core in (0, 1):
                send(si.at[core, r], iz.at[k, t], s_iz, r_iz.at[c], dev(d, 0, 0, core))
        else:
            send(si.at[1 - k, r], iz.at[k, t], s_iz, r_iz.at[c], sib)
            local(si.at[k, r], iz.at[k, t], r_iz.at[c])

    def each(step, c, g):
        for s in GROUPS[g]:
            step(c, s)

    def finish_weights():
        wait(gwo, r_w.at[0])
        wait(uwo, r_w.at[1])
        wait(dwo, r_w.at[2])
        keep_weights(1 - k, gwo, uwo, dwo)

    def swap_inputs():
        send(ta.at[1 - k], to, s_to.at[0], r_to.at[0], sib)
        send(gb.at[1 - k], go, s_to.at[1], r_to.at[1], sib)

    def begin():
        masks()
        keep_weights(k, gw, uw, dw)

    steps = {
        "A": start_tokens,
        "G": start_grads,
        "F": lambda c, g: each(forward_tokens, c, g),
        "B": lambda c, g: each(forward_grads, c, g),
        "P": lambda c, g: stage1(c, GROUPS[g]),
        "E": lambda c, g: each(elementwise, c, g),
        "S": lambda c, g: each(share, c, g),
        "Q": lambda c, g: stage2(c, GROUPS[g]),
        "I": lambda c, g: each(send_inputs, c, g),
        "Z": lambda c, g: each(pass_mixed, c, g),
        "R": lambda c, g: each(reduce_inputs, c, g),
        "W": start_weights,
        "M": begin,
        "N": finish_weights,
        "X": swap_inputs,
    }
    for line in ORDER:
        for step in line.split():
            steps[step[0]](*map(int, step[1:]))

    wait(to, r_to.at[0])
    wait(go, r_to.at[1])
    wait(ho, r_ho)
    own = pl.ds(pl.multiple_of(k * FC, FC), FC)
    for i, out in enumerate((gg_o, ug_o)):
        c = slice(i * U, (i + 1) * U)
        out[...] = (tn(hd[:, c], ta[k]) + tn(ho[:, c], to[...])) * keep[i, :, own].astype(F32)
    c = slice(2 * U, 3 * U)
    dg_o[...] = (tn(hd[:, c], gb[k]) + tn(ho[:, c], go[...])) * keep[2, :, own].astype(F32)

    for c in range(NC):
        wait(mx.at[c], r_mx.at[c])
        for core in (0, 1):
            part = [mx[c, core, i * T : (i + 1) * T, :] for i in range(NX)]
            there = slice(core * H + c * T, core * H + (c + 1) * T)
            mixed_o[there, :] = ((part[0] + part[1]) + (part[2] + part[3])).astype(BF)
    for c in range(NC):
        wait(iz.at[:, pl.ds(c * NZ * T, NZ * T)], r_iz.at[c])
        for core in (0, 1):
            part = [iz[core, (c * NZ + i) * T : (c * NZ + i + 1) * T, :].astype(F32) for i in range(NZ)]
            low = (part[0] + part[1]) + (part[2] + part[3])
            high = (part[4] + part[5]) + (part[6] + part[7])
            there = slice(core * H + c * T, core * H + (c + 1) * T)
            ig_o[there, :] = (low + high).astype(BF)

    wait(ta.at[0, pl.ds(0, 7 * NC * T)], s_ax)
    wait(ta.at[0, pl.ds(0, 5 * NC * T)], s_bz)
    wait(gb.at[:, pl.ds(0, 4 * NC * T)], s_bh.at[0])
    wait(gb.at[0, pl.ds(0, 2 * NC * T)], s_bh.at[1])
    for i in range(3):
        wait((gwo, uwo, dwo)[i], s_w.at[i])
        wait(gb.at[:, pl.ds(0, NS * T)], s_bx.at[i])
        wait(pp.at[pl.ds(0, NS * T)], s_ry.at[i])
        wait(hd.at[pl.ds(0, NS * T)], s_ay.at[i])
        wait(p2.at[pl.ds(0, NS * T)], s_ix.at[i])
    for j in (0, 1):
        wait(ta.at[j, pl.ds(0, 7 * NC * S)], s_az.at[j])
        wait(to, s_to.at[j])
        wait(mz.at[pl.ds(0, 3 * NC * S)], s_mz.at[j])
        wait(mz.at[pl.ds(0, NC * S), 0:FC], s_mzh.at[j])
    wait(ho, s_ho)
    wait(gb.at[0, pl.ds(0, 15 * NC * T)], s_iz)
    wait(ta.at[:, pl.ds(0, 7 * NC * T)], s_mx)


def per_device(tokens, gate_weight, up_weight, down_weight, gate_mask, up_mask, down_mask, out_grad):
    vmem = pl.BlockSpec(memory_space=pltpu.VMEM)
    dma = pltpu.SemaphoreType.DMA
    v = pltpu.VMEM
    mixed, input_grad, gate_grad, up_grad, down_grad = pl.pallas_call(
        kernel,
        out_shape=(
            jax.ShapeDtypeStruct((2 * H, FC), BF),
            jax.ShapeDtypeStruct((2 * H, FC), BF),
            jax.ShapeDtypeStruct((U, FC), F32),
            jax.ShapeDtypeStruct((U, FC), F32),
            jax.ShapeDtypeStruct((U, FC), F32),
        ),
        in_specs=[vmem] * 8,
        out_specs=(vmem,) * 5,
        scratch_shapes=[
            v((2, NS * S, FC), BF),
            v((2, NS * S, FC), BF),
            v((NS * S, FC), BF),
            v((NS * S, FC), BF),
            v((U, FC), BF),
            v((U, FC), BF),
            v((U, FC), BF),
            v((2 * U, F), BF),
            v((UP, F), BF),
            v((3, U, F), BF),
            v((NS * S, W), F32),
            v((NS * S, W), BF),
            v((3, NS * T, W), BF),
            v((NS * S, W), BF),
            v((NS * S, W), BF),
            v((NS * S, F), F32),
            v((NS * S, F), BF),
            v((NS * S, F), BF),
            v((NC, 2, S, F), BF),
            v((NS * S, F), BF),
            v((3, NS * T, F), BF),
            v((2, NS * T, FC), BF),
            v((2, NS * T, FC), BF),
            v((NC, 2, S, FC), F32),
            v((NC, 2, S, FC), F32),
            dma, dma, dma((3,)), dma((3,)), dma((2,)), dma((2,)), dma((3,)), dma((3,)), dma, dma((2,)), dma((2,)), dma((2,)), dma((3,)), dma, dma,
            dma((NC,)), dma((NC, 8)), dma((3,)), dma((NC, 8)), dma((NC, 8, 2)), dma((NC, 8)), dma((NC, 8)), dma, dma((2,)), dma((NC, 8)), dma((NC, 8)), dma((NC,)), dma((NC,)),
        ],
        compiler_params=pltpu.CompilerParams(
            collective_id=0, has_side_effects=True, vmem_limit_bytes=60 << 20
        ),
        cost_estimate=pl.CostEstimate(flops=9_000_000_000, bytes_accessed=8 << 20, transcendentals=120_000),
        name="sublayer",
    )(tokens, gate_weight.T, up_weight.T, down_weight, gate_mask, up_mask, down_mask.T, out_grad)
    return mixed, input_grad, gate_grad.T, up_grad.T, down_grad


def solution(mesh):
    return jax.shard_map(
        per_device,
        mesh=mesh,
        in_specs=(
            P("row", "col"), P("col", "row"), P("col", "row"), P("row", "col"), P(), P(), P(), P("row", "col"),
        ),
        out_specs=(P("row", "col"), P("row", "col"), P("col", "row"), P("col", "row"), P("row", "col")),
        check_vma=False,
    )
```

time: 789 us -> 113 us (0.14)
  waiting for transfers between devices: 726 us -> 0 us
  Pallas kernels: 0 us -> 105 us
  matrix products: 34.4 us -> 0 us
  between operations: 14.2 us -> 0.66 us
  other arithmetic: 8.8 us -> 0 us
    reduce_scatter x4 -> x0, waiting for transfers between devices: 515 us -> none  [the longest x1 222 us: per_device(): lax.psum_scatter(contract_last(block, kept_both), 'row', scatter_dimensio...]
    all_gather x4 -> x0, waiting for transfers between devices: 209 us -> none  [the longest x1 78.1 us: per_device(): grad_all = lax.all_gather(out_grad, 'row', axis=0, tiled=True)]
    pallas_call x0 -> x1, Pallas kernels: none -> 105 us  [per_device(): pl.pallas_call(kernel, out_shape=(jax.ShapeDtypeStruct((2 * H, FC), BF),...]
    dot_general x12 -> x0, matrix products: 34.4 us -> none  [the longest x2 11.3 us: contract_last(): lax.dot_general(left, right, (((1,), (1,)), ((), ())), preferred_element_...]
  transfers between devices with their start and end apart: 8 -> 0, of which waited for: 8 -> 0; matrix products, arithmetic and copies ran while one was open for 5% -> 0% of each run, Pallas kernels for 0% -> 0%
where the time goes in v2:
time: 113 us; the launch traced here: 112 us
  Pallas kernels  105 us (93%)
  local copies, waits for them, and re-layouts  6.81 us (6%)
    pallas_call x1, Pallas kernels, per_device(): pl.pallas_call(kernel, out_shape=(jax.ShapeDtypeStruct((2 * H, FC), BF),...  105 us
    unnamed x11, local copies, waits for them, and re-layouts  6.81 us

profile of v2, /device:TPU:1, one launch (start us, length us, event | category | flops | bytes accessed | tf_op | source)
XLA Modules:
  0.0 112.4 jit_solution(8077971899024854394)
XLA Ops:
  0.6 104.9 %sublayer.1 = (bf16[64,512]{1,0:T(8,128)(2,1)}, bf16[64,512]{1,0:T(8,128)(2,1)}, f32[448,512]{1,0:T(8,128)}, f32[448,512]{1,0:T(8,128)}, f32[448,512]{1,0:T(8,128)}) custom-call(bf16[64,512]{1,0:T(8,128)(2,1)} %tok.1, bf16[448,512]{1,0:T(8,128)(2,1)} %bitcast.7, bf16[448,512]{1,0:T(8,128)(2,1)} %bitcast.8, bf16[448,512]{1,0:T(8,128)(2,1)} %dw.1, ...), custom_call_target="tpu_custom_call" | custom-call | flops 8999999488 | bytes 8388608 | tf_op jit(solution)/shard_map/sublayer/pallas_call | solution.py:377
  105.5 0.0 copy-start.2
  105.5 1.5 %copy.18 = bf16[64,512]{1,0:T(8,128)(2,1)} copy(bf16[64,512]{1,0:T(8,128)(2,1)} %get-tuple-element.20) | data formatting | bytes 131072
  107.0 0.0 copy-done.2
  107.0 0.6 copy.19
  107.7 0.0 copy-start.1
  107.7 2.2 %copy.20 = f32[512,448]{0,1:T(8,128)} copy(f32[512,448]{0,1:T(8,128)} %bitcast.6) | data formatting | bytes 1835008
  109.9 0.0 copy-done.1
  109.9 0.0 copy-start
  109.9 0.9 copy.21
  110.8 0.6 copy-done
  111.4 0.9 copy.22
Async XLA Ops:
  105.5 1.5 %copy-start.2 = (bf16[64,512]{1,0:T(8,128)(2,1)S(1)}, bf16[64,512]{1,0:T(8,128)(2,1)}, u32[]{:S(2)}) copy-start(bf16[64,512]{1,0:T(8,128)(2,1)} %get-tuple-element.21) | copy-start | bytes 196612
  107.7 2.2 %copy-start.1 = (f32[448,512]{1,0:T(8,128)S(1)}, f32[448,512]{1,0:T(8,128)}, u32[]{:S(2)}) copy-start(f32[448,512]{1,0:T(8,128)} %get-tuple-element.13) | copy-start | bytes 2752516
  109.9 1.5 %copy-start = (f32[448,512]{1,0:T(8,128)S(1)}, f32[448,512]{1,0:T(8,128)}, u32[]{:S(2)}) copy-start(f32[448,512]{1,0:T(8,128)} %get-tuple-element.24) | copy-start | bytes 2752516

commit v3 on v2

--- a/solution.py
+++ b/solution.py
@@ -19,35 +19,41 @@
 U = 448
 UP = 512
 W = 2 * U + UP
+CUT = 640
 DZ = (0, 1, -1, 2, -2, 3, -3, 4)
 SLOT = {d % NZ: i for i, d in enumerate(DZ)}
 GROUPS = ((0,), (1, 2), (3, 4), (5, 6), (7,))
 ORDER = (
-    "A0 G0 A1 W",
-    "B00 G1 M B01",
-    "F00 N B02 P00",
-    "F01 B03 P01 F02",
-    "P02 B04 F10 B10",
-    "F03 P03 B11 F04",
-    "P04 E02 E01 B12",
-    "F11 S02 E04 S04",
-    "E03 F12 S03 B13",
-    "E00 P12 F13 Q04",
-    "Q03 S01 B14 P11",
-    "Q02 Z04 F14 P14",
-    "Z03 P13 I03 E12",
-    "I04 E14 S14 S00",
-    "Z02 I02 E13 S13",
-    "Q01 E11 Z01 Q14",
-    "I01 S12 I14 P10",
-    "Q00 Z14 I00 Q13",
-    "Z13 I13 R02 S11",
-    "Z00 Q12 Z12 E10",
-    "R01 I12 S10 X",
-    "R04 Q11 I11 Z11",
-    "Q10 R14 R13 I10",
-    "R00 Z10 R03 R12",
-    "R10 R11",
+    "G0 A0 A1 G1",
+    "M W B01 B00",
+    "B10 B11 F00 F10",
+    "N B02 F01 P01",
+    "P00 P10 F11 B12",
+    "Y01 B03 P11 F02",
+    "Y10 Y00 P02 F12",
+    "Y11 B13 P12 E00",
+    "Y02 B04 F03 S00",
+    "E11 P03 Y12 F13",
+    "P13 B14 F04 P04",
+    "E01 V00 Y03 Y04",
+    "F14 P14 E12 Y13",
+    "E04 S04 S01 X",
+    "E02 Y14 E03 V04",
+    "Q00 E10 S03 E13",
+    "S13 E14 Q04 I00",
+    "S14 I04 V03 S02",
+    "Z04 V14 V13 V01",
+    "Q03 I03 Z03 V02",
+    "S12 S11 Q14 R04",
+    "Z14 I14 Q13 I13",
+    "Q02 I02 Z02 V11",
+    "Z13 V12 Q01 I01",
+    "S10 Z01 Q11 I11",
+    "R00 V10 Q12 Z12",
+    "I12 R01 Z00 R14",
+    "Z11 Q10 R12 R13",
+    "R03 R11 I10 Z10",
+    "R10 R02",
 )
 BF = jnp.bfloat16
 F32 = jnp.float32
@@ -70,9 +76,9 @@
     tok, gw, uw, dw, gm, um, dm, og,
     mixed_o, ig_o, gg_o, ug_o, dg_o,
     ta, gb, to, go, gwo, uwo, dwo, wgu, kd, keep,
-    pf, pp, pr, hd, ho, mp, mz, mr, mr0, p2, ir, si, iz, sm, mx,
-    s_ax, s_bz, s_w, s_bx, s_bh, s_az, s_ry, s_ay, s_ho, s_to, s_mz, s_mzh, s_ix, s_iz, s_mx,
-    r_ax, r_bz, r_w, r_bx, r_az, r_ry, r_ay, r_ho, r_to, r_mz, r_ix, r_iz, r_mx,
+    pf, pp, ph, pr, hd, ho, mp, mz, mr, mr0, p2, ir, si, iz, sm, mx,
+    s_ax, s_bz, s_w, s_bx, s_bh, s_az, s_rh, s_ry, s_ay, s_av, s_ho, s_to, s_mz, s_mzh, s_ix, s_iz, s_mx,
+    r_ax, r_bz, r_w, r_bx, r_az, r_rh, r_ry, r_ay, r_av, r_ho, r_to, r_mz, r_ix, r_iz, r_mx,
 ):
     row, col = lax.axis_index("row"), lax.axis_index("col")
     z, x = row // NX, row % NX
@@ -180,6 +186,8 @@
         kd[0:U, c] = keep[2, :, c] * d_ref[...]
         kd[U:UP, c] = jnp.zeros((UP - U, FC), BF)
 
+    halves = (slice(0, CUT), slice(CUT, W))
+
     def stage1(c, slots):
         r = pl.ds((c * NZ + slots[0]) * S, len(slots) * S)
         for s in slots:
@@ -192,16 +200,25 @@
         pp[r, 2 * U : W] = back.astype(BF)
         for s in slots:
             g = c * NZ + s
-            for e in (1, 3, 2):
-                other = (y + e) % NY
-                send(pp.at[rows(g * S + other * T, T)], pr.at[e - 1, pl.ds(g * T, T)], s_ry.at[e - 1], r_ry.at[c, s], dev(0, 0, e, k))
+            far = rows(g * S + (y + 2) % NY * T, T)
+            for way, cols in enumerate(halves):
+                send(pp.at[far, cols], ph.at[pl.ds(g * T, T), cols], s_rh.at[way], r_rh.at[c, s], dev(0, 0, 1 - 2 * way, k))
+
+    def pass_sums(c, s):
+        g = c * NZ + s
+        r = pl.ds(g * T, T)
+        wait(pp.at[pl.ds(0, T)], r_rh.at[c, s])
+        for way, cols in enumerate(halves):
+            there = rows(g * S + (y + 1 + 2 * way) % NY * T, T)
+            pp[there, cols] = (pf[there, cols] + ph[r, cols].astype(F32)).astype(BF)
+            send(pp.at[there], pr.at[way, r], s_ry.at[way], r_ry.at[c, s], dev(0, 0, 1 - 2 * way, k))
 
     def elementwise(c, s):
         g = c * NZ + s
-        wait(pp.at[pl.ds(0, 3 * T)], r_ry.at[c, s])
+        wait(pp.at[pl.ds(0, 2 * T)], r_ry.at[c, s])
         mine = rows(g * S + y * T, T)
         r = pl.ds(g * T, T)
-        tot = (pf[mine, :] + pr[0, r, :].astype(F32)) + (pr[1, r, :].astype(F32) + pr[2, r, :].astype(F32))
+        tot = pf[mine, :] + (pr[0, r, :].astype(F32) + pr[1, r, :].astype(F32))
         gate, up, hg = tot[:, 0:U], tot[:, U : 2 * U], tot[:, 2 * U : 3 * U]
         sig = 1.0 / (1.0 + jnp.exp(-gate))
         act = gate * sig
@@ -212,13 +229,20 @@
     def share(c, s):
         g = c * NZ + s
         mine = rows(g * S + y * T, T)
-        for e in (1, 3, 2):
-            send(hd.at[mine], hd.at[mine], s_ay.at[e - 1], r_ay.at[c, s], dev(0, 0, e, k))
+        for way in (0, 1):
+            send(hd.at[mine], hd.at[mine], s_ay.at[way], r_ay.at[c, s, way], dev(0, 0, 1 - 2 * way, k))
+
+    def share_on(c, s):
+        g = c * NZ + s
+        for way, cols in enumerate(halves):
+            there = rows(g * S + (y + 3 - 2 * way) % NY * T, T)
+            wait(hd.at[there], r_ay.at[c, s, way])
+            send(hd.at[there, cols], hd.at[there, cols], s_av.at[way], r_av.at[c, s], dev(0, 0, 1 - 2 * way, k))
 
     def stage2(c, slots):
         r = pl.ds((c * NZ + slots[0]) * S, len(slots) * S)
         for s in slots:
-            wait(hd.at[pl.ds(0, 3 * T)], r_ay.at[c, s])
+            wait(hd.at[pl.ds(0, T)], r_av.at[c, s])
         mp[r, :] = nn(hd[r, 2 * U : W], kd[...])
         p2[r, :] = nn(hd[r, 0 : 2 * U], wgu[...]).astype(BF)
         send(hd.at[r], ho.at[r], s_ho, r_ho, sib)
@@ -310,6 +334,8 @@
         "F": lambda c, g: each(forward_tokens, c, g),
         "B": lambda c, g: each(forward_grads, c, g),
         "P": lambda c, g: stage1(c, GROUPS[g]),
+        "Y": lambda c, g: each(pass_sums, c, g),
+        "V": lambda c, g: each(share_on, c, g),
         "E": lambda c, g: each(elementwise, c, g),
         "S": lambda c, g: each(share, c, g),
         "Q": lambda c, g: stage2(c, GROUPS[g]),
@@ -357,11 +383,13 @@
     for i in range(3):
         wait((gwo, uwo, dwo)[i], s_w.at[i])
         wait(gb.at[:, pl.ds(0, NS * T)], s_bx.at[i])
-        wait(pp.at[pl.ds(0, NS * T)], s_ry.at[i])
-        wait(hd.at[pl.ds(0, NS * T)], s_ay.at[i])
         wait(p2.at[pl.ds(0, NS * T)], s_ix.at[i])
     for j in (0, 1):
         wait(ta.at[j, pl.ds(0, 7 * NC * S)], s_az.at[j])
+        wait(pp.at[pl.ds(0, NS * T)], s_ry.at[j])
+        wait(hd.at[pl.ds(0, NS * T)], s_ay.at[j])
+        wait(pp.at[pl.ds(0, NS * T), halves[j]], s_rh.at[j])
+        wait(hd.at[pl.ds(0, NS * T), halves[j]], s_av.at[j])
         wait(to, s_to.at[j])
         wait(mz.at[pl.ds(0, 3 * NC * S)], s_mz.at[j])
         wait(mz.at[pl.ds(0, NC * S), 0:FC], s_mzh.at[j])
@@ -398,7 +426,8 @@
             v((3, U, F), BF),
             v((NS * S, W), F32),
             v((NS * S, W), BF),
-            v((3, NS * T, W), BF),
+            v((NS * T, W), BF),
+            v((2, NS * T, W), BF),
             v((NS * S, W), BF),
             v((NS * S, W), BF),
             v((NS * S, F), F32),
@@ -411,8 +440,8 @@
             v((2, NS * T, FC), BF),
             v((NC, 2, S, FC), F32),
             v((NC, 2, S, FC), F32),
-            dma, dma, dma((3,)), dma((3,)), dma((2,)), dma((2,)), dma((3,)), dma((3,)), dma, dma((2,)), dma((2,)), dma((2,)), dma((3,)), dma, dma,
-            dma((NC,)), dma((NC, 8)), dma((3,)), dma((NC, 8)), dma((NC, 8, 2)), dma((NC, 8)), dma((NC, 8)), dma, dma((2,)), dma((NC, 8)), dma((NC, 8)), dma((NC,)), dma((NC,)),
+            dma, dma, dma((3,)), dma((3,)), dma((2,)), dma((2,)), dma((2,)), dma((2,)), dma((2,)), dma((2,)), dma, dma((2,)), dma((2,)), dma((2,)), dma((3,)), dma, dma,
+            dma((NC,)), dma((NC, 8)), dma((3,)), dma((NC, 8)), dma((NC, 8, 2)), dma((NC, 8)), dma((NC, 8)), dma((NC, 8, 2)), dma((NC, 8)), dma, dma((2,)), dma((NC, 8)), dma((NC, 8)), dma((NC,)), dma((NC,)),
         ],
         compiler_params=pltpu.CompilerParams(
             collective_id=0, has_side_effects=True, vmem_limit_bytes=60 << 20

time: 113 us -> 106 us (0.938)
  Pallas kernels: 105 us -> 98.2 us
    pallas_call x1, Pallas kernels: 105 us -> 98.2 us  [per_device(): pl.pallas_call(kernel, out_shape=(jax.ShapeDtypeStruct((2 * H, FC), BF),...]
where the time goes in v3:
time: 106 us
  Pallas kernels  98.2 us (93%)
  local copies, waits for them, and re-layouts  6.81 us (6%)
    pallas_call x1, Pallas kernels, per_device(): pl.pallas_call(kernel, out_shape=(jax.ShapeDtypeStruct((2 * H, FC), BF),...  98.2 us
    unnamed x11, local copies, waits for them, and re-layouts  6.81 us

profile of v3, /device:TPU:1, one launch (start us, length us, event | category | flops | bytes accessed | tf_op | source)
XLA Modules:
  0.0 105.6 jit_solution(427954373387211358)
XLA Ops:
  0.6 98.2 %sublayer.1 = (bf16[64,512]{1,0:T(8,128)(2,1)}, bf16[64,512]{1,0:T(8,128)(2,1)}, f32[448,512]{1,0:T(8,128)}, f32[448,512]{1,0:T(8,128)}, f32[448,512]{1,0:T(8,128)}) custom-call(bf16[64,512]{1,0:T(8,128)(2,1)} %tok.1, bf16[448,512]{1,0:T(8,128)(2,1)} %bitcast.7, bf16[448,512]{1,0:T(8,128)(2,1)} %bitcast.8, bf16[448,512]{1,0:T(8,128)(2,1)} %dw.1, ...), custom_call_target="tpu_custom_call" | custom-call | flops 8999999488 | bytes 8388608 | tf_op jit(solution)/shard_map/sublayer/pallas_call | solution.py:405
  98.8 0.0 copy-start.2
  98.8 1.5 %copy.18 = bf16[64,512]{1,0:T(8,128)(2,1)} copy(bf16[64,512]{1,0:T(8,128)(2,1)} %get-tuple-element.20) | data formatting | bytes 131072
  100.3 0.0 copy-done.2
  100.3 0.6 copy.19
  101.0 0.0 copy-start.1
  101.0 2.2 %copy.20 = f32[512,448]{0,1:T(8,128)} copy(f32[512,448]{0,1:T(8,128)} %bitcast.6) | data formatting | bytes 1835008
  103.2 0.0 copy-done.1
  103.2 0.0 copy-start
  103.2 0.9 copy.21
  104.1 0.6 copy-done
  104.7 0.9 copy.22
Async XLA Ops:
  98.8 1.5 %copy-start.2 = (bf16[64,512]{1,0:T(8,128)(2,1)S(1)}, bf16[64,512]{1,0:T(8,128)(2,1)}, u32[]{:S(2)}) copy-start(bf16[64,512]{1,0:T(8,128)(2,1)} %get-tuple-element.21) | copy-start | bytes 196612
  101.0 2.2 %copy-start.1 = (f32[448,512]{1,0:T(8,128)S(1)}, f32[448,512]{1,0:T(8,128)}, u32[]{:S(2)}) copy-start(f32[448,512]{1,0:T(8,128)} %get-tuple-element.13) | copy-start | bytes 2752516
  103.2 1.5 %copy-start = (f32[448,512]{1,0:T(8,128)S(1)}, f32[448,512]{1,0:T(8,128)}, u32[]{:S(2)}) copy-start(f32[448,512]{1,0:T(8,128)} %get-tuple-element.24) | copy-start | bytes 2752516

commit v4 on v3

--- a/solution.py
+++ b/solution.py
@@ -24,36 +24,36 @@
 SLOT = {d % NZ: i for i, d in enumerate(DZ)}
 GROUPS = ((0,), (1, 2), (3, 4), (5, 6), (7,))
 ORDER = (
-    "G0 A0 A1 G1",
-    "M W B01 B00",
-    "B10 B11 F00 F10",
-    "N B02 F01 P01",
-    "P00 P10 F11 B12",
-    "Y01 B03 P11 F02",
-    "Y10 Y00 P02 F12",
-    "Y11 B13 P12 E00",
-    "Y02 B04 F03 S00",
-    "E11 P03 Y12 F13",
-    "P13 B14 F04 P04",
-    "E01 V00 Y03 Y04",
-    "F14 P14 E12 Y13",
-    "E04 S04 S01 X",
-    "E02 Y14 E03 V04",
-    "Q00 E10 S03 E13",
-    "S13 E14 Q04 I00",
-    "S14 I04 V03 S02",
-    "Z04 V14 V13 V01",
-    "Q03 I03 Z03 V02",
-    "S12 S11 Q14 R04",
-    "Z14 I14 Q13 I13",
-    "Q02 I02 Z02 V11",
-    "Z13 V12 Q01 I01",
-    "S10 Z01 Q11 I11",
-    "R00 V10 Q12 Z12",
-    "I12 R01 Z00 R14",
-    "Z11 Q10 R12 R13",
-    "R03 R11 I10 Z10",
-    "R10 R02",
+    "A0 G0 A1 G1",
+    "B10 W B01 B11",
+    "F00 M F10 B02",
+    "N P10 F01 P01",
+    "B12 F11 Y10 P11",
+    "B03 Y01 E10 S10",
+    "F02 P02 Y11 F12",
+    "V10 P12 B04 B13",
+    "Y02 F03 P03 Y12",
+    "F13 E02 B00 S02",
+    "B14 F04 E01 P04",
+    "Y03 F14 P13 V02",
+    "E12 P14 Q10 Y04",
+    "Y13 E03 Y14 E04",
+    "S04 S03 E14 S14",
+    "V04 E13 S13 Q02",
+    "I10 I02 V14 V03",
+    "P00 Q04 Z04 S01",
+    "I04 Q14 I14 Z14",
+    "V13 Q03 I03 S12",
+    "Y00 Z03 V01 E11",
+    "Q13 Z13 V12 I13",
+    "S11 E00 S00 Z02",
+    "Q01 R10 I01 Q12",
+    "Z12 V11 I12 V00",
+    "Z01 Q11 I11 R14",
+    "X Z11 Q00 R13",
+    "I00 R04 R03 R12",
+    "R02 R01 Z00 Z10",
+    "R00 R11",
 )
 BF = jnp.bfloat16
 F32 = jnp.float32

time: 106 us -> 104 us (0.981)
  Pallas kernels: 98.2 us -> 96.6 us
    pallas_call x1, Pallas kernels: 98.2 us -> 96.6 us  [per_device(): pl.pallas_call(kernel, out_shape=(jax.ShapeDtypeStruct((2 * H, FC), BF),...]
where the time goes in v4:
time: 104 us
  Pallas kernels  96.6 us (93%)
  local copies, waits for them, and re-layouts  6.81 us (7%)
    pallas_call x1, Pallas kernels, per_device(): pl.pallas_call(kernel, out_shape=(jax.ShapeDtypeStruct((2 * H, FC), BF),...  96.6 us
    unnamed x11, local copies, waits for them, and re-layouts  6.81 us

profile of v4, /device:TPU:1, one launch (start us, length us, event | category | flops | bytes accessed | tf_op | source)
XLA Modules:
  0.0 104.0 jit_solution(3188258435081601871)
XLA Ops:
  0.6 96.6 %sublayer.1 = (bf16[64,512]{1,0:T(8,128)(2,1)}, bf16[64,512]{1,0:T(8,128)(2,1)}, f32[448,512]{1,0:T(8,128)}, f32[448,512]{1,0:T(8,128)}, f32[448,512]{1,0:T(8,128)}) custom-call(bf16[64,512]{1,0:T(8,128)(2,1)} %tok.1, bf16[448,512]{1,0:T(8,128)(2,1)} %bitcast.7, bf16[448,512]{1,0:T(8,128)(2,1)} %bitcast.8, bf16[448,512]{1,0:T(8,128)(2,1)} %dw.1, ...), custom_call_target="tpu_custom_call" | custom-call | flops 8999999488 | bytes 8388608 | tf_op jit(solution)/shard_map/sublayer/pallas_call | solution.py:405
  97.2 0.0 copy-start.2
  97.2 1.5 %copy.18 = bf16[64,512]{1,0:T(8,128)(2,1)} copy(bf16[64,512]{1,0:T(8,128)(2,1)} %get-tuple-element.20) | data formatting | bytes 131072
  98.7 0.0 copy-done.2
  98.7 0.6 copy.19
  99.4 0.0 copy-start.1
  99.4 2.2 %copy.20 = f32[512,448]{0,1:T(8,128)} copy(f32[512,448]{0,1:T(8,128)} %bitcast.6) | data formatting | bytes 1835008
  101.6 0.0 copy-done.1
  101.6 0.0 copy-start
  101.6 0.9 copy.21
  102.5 0.6 copy-done
  103.1 0.9 copy.22
Async XLA Ops:
  97.2 1.5 %copy-start.2 = (bf16[64,512]{1,0:T(8,128)(2,1)S(1)}, bf16[64,512]{1,0:T(8,128)(2,1)}, u32[]{:S(2)}) copy-start(bf16[64,512]{1,0:T(8,128)(2,1)} %get-tuple-element.21) | copy-start | bytes 196612
  99.4 2.2 %copy-start.1 = (f32[448,512]{1,0:T(8,128)S(1)}, f32[448,512]{1,0:T(8,128)}, u32[]{:S(2)}) copy-start(f32[448,512]{1,0:T(8,128)} %get-tuple-element.13) | copy-start | bytes 2752516
  101.6 1.5 %copy-start = (f32[448,512]{1,0:T(8,128)S(1)}, f32[448,512]{1,0:T(8,128)}, u32[]{:S(2)}) copy-start(f32[448,512]{1,0:T(8,128)} %get-tuple-element.24) | copy-start | bytes 2752516

commit v5 on v4

--- a/solution.py
+++ b/solution.py
@@ -76,9 +76,10 @@
     tok, gw, uw, dw, gm, um, dm, og,
     mixed_o, ig_o, gg_o, ug_o, dg_o,
     ta, gb, to, go, gwo, uwo, dwo, wgu, kd, keep,
-    pf, pp, ph, pr, hd, ho, mp, mz, mr, mr0, p2, ir, si, iz, sm, mx,
+    pf, pp, ph, pr, hd, ho, mp, mz, mr, mr0, p2, ir, si, iz, sm, mx, gwv, uwv, dwv, gv,
     s_ax, s_bz, s_w, s_bx, s_bh, s_az, s_rh, s_ry, s_ay, s_av, s_ho, s_to, s_mz, s_mzh, s_ix, s_iz, s_mx,
     r_ax, r_bz, r_w, r_bx, r_az, r_rh, r_ry, r_ay, r_av, r_ho, r_to, r_mz, r_ix, r_iz, r_mx,
+    l_w, l_o,
 ):
     row, col = lax.axis_index("row"), lax.axis_index("col")
     z, x = row // NX, row % NX
@@ -103,6 +104,10 @@
 
     def rows(start, size):
         return pl.ds(pl.multiple_of(start, 16), size)
+
+    local(gw, gwv, l_w.at[0])
+    local(uw, uwv, l_w.at[1])
+    local(dw, dwv, l_w.at[2])
 
     bar = pltpu.get_barrier_semaphore()
     partners = [sib]
@@ -326,7 +331,10 @@
 
     def begin():
         masks()
-        keep_weights(k, gw, uw, dw)
+        wait(gwv, l_w.at[0])
+        wait(uwv, l_w.at[1])
+        wait(dwv, l_w.at[2])
+        keep_weights(k, gwv, uwv, dwv)
 
     steps = {
         "A": start_tokens,
@@ -357,9 +365,11 @@
     own = pl.ds(pl.multiple_of(k * FC, FC), FC)
     for i, out in enumerate((gg_o, ug_o)):
         c = slice(i * U, (i + 1) * U)
-        out[...] = (tn(hd[:, c], ta[k]) + tn(ho[:, c], to[...])) * keep[i, :, own].astype(F32)
+        gv[i] = (tn(hd[:, c], ta[k]) + tn(ho[:, c], to[...])) * keep[i, :, own].astype(F32)
+        local(gv.at[i], out, l_o.at[i])
     c = slice(2 * U, 3 * U)
-    dg_o[...] = (tn(hd[:, c], gb[k]) + tn(ho[:, c], go[...])) * keep[2, :, own].astype(F32)
+    gv[2] = (tn(hd[:, c], gb[k]) + tn(ho[:, c], go[...])) * keep[2, :, own].astype(F32)
+    local(gv.at[2], dg_o, l_o.at[2])
 
     for c in range(NC):
         wait(mx.at[c], r_mx.at[c])
@@ -376,6 +386,8 @@
             there = slice(core * H + c * T, core * H + (c + 1) * T)
             ig_o[there, :] = (low + high).astype(BF)
 
+    for i in range(3):
+        wait(gv.at[i], l_o.at[i])
     wait(ta.at[0, pl.ds(0, 7 * NC * T)], s_ax)
     wait(ta.at[0, pl.ds(0, 5 * NC * T)], s_bz)
     wait(gb.at[:, pl.ds(0, 4 * NC * T)], s_bh.at[0])
@@ -400,6 +412,7 @@
 
 def per_device(tokens, gate_weight, up_weight, down_weight, gate_mask, up_mask, down_mask, out_grad):
     vmem = pl.BlockSpec(memory_space=pltpu.VMEM)
+    hbm = pl.BlockSpec(memory_space=pl.ANY)
     dma = pltpu.SemaphoreType.DMA
     v = pltpu.VMEM
     mixed, input_grad, gate_grad, up_grad, down_grad = pl.pallas_call(
@@ -411,8 +424,8 @@
             jax.ShapeDtypeStruct((U, FC), F32),
             jax.ShapeDtypeStruct((U, FC), F32),
         ),
-        in_specs=[vmem] * 8,
-        out_specs=(vmem,) * 5,
+        in_specs=[vmem, hbm, hbm, hbm, vmem, vmem, vmem, vmem],
+        out_specs=(vmem, vmem, hbm, hbm, hbm),
         scratch_shapes=[
             v((2, NS * S, FC), BF),
             v((2, NS * S, FC), BF),
@@ -440,8 +453,13 @@
             v((2, NS * T, FC), BF),
             v((NC, 2, S, FC), F32),
             v((NC, 2, S, FC), F32),
+            v((U, FC), BF),
+            v((U, FC), BF),
+            v((U, FC), BF),
+            v((3, U, FC), F32),
             dma, dma, dma((3,)), dma((3,)), dma((2,)), dma((2,)), dma((2,)), dma((2,)), dma((2,)), dma((2,)), dma, dma((2,)), dma((2,)), dma((2,)), dma((3,)), dma, dma,
             dma((NC,)), dma((NC, 8)), dma((3,)), dma((NC, 8)), dma((NC, 8, 2)), dma((NC, 8)), dma((NC, 8)), dma((NC, 8, 2)), dma((NC, 8)), dma, dma((2,)), dma((NC, 8)), dma((NC, 8)), dma((NC,)), dma((NC,)),
+            dma((3,)), dma((3,)),
         ],
         compiler_params=pltpu.CompilerParams(
             collective_id=0, has_side_effects=True, vmem_limit_bytes=60 << 20

time: 104 us -> 103 us (level)
  Pallas kernels: 96.6 us -> 95 us
    pallas_call x1, Pallas kernels: 96.6 us -> 95 us  [per_device(): pl.pallas_call(kernel, out_shape=(jax.ShapeDtypeStruct((2 * H, FC), BF),...]
where the time goes in v5:
time: 103 us; the launch traced here: 102 us
  Pallas kernels  95 us (92%)
  local copies, waits for them, and re-layouts  6.81 us (7%)
    pallas_call x1, Pallas kernels, per_device(): pl.pallas_call(kernel, out_shape=(jax.ShapeDtypeStruct((2 * H, FC), BF),...  95 us
    unnamed x11, local copies, waits for them, and re-layouts  6.81 us

profile of v5, /device:TPU:1, one launch (start us, length us, event | category | flops | bytes accessed | tf_op | source)
XLA Modules:
  0.0 102.4 jit_solution(13985592984452435523)
XLA Ops:
  0.6 95.0 %sublayer.1 = (bf16[64,512]{1,0:T(8,128)(2,1)}, bf16[64,512]{1,0:T(8,128)(2,1)}, f32[448,512]{1,0:T(8,128)}, f32[448,512]{1,0:T(8,128)}, f32[448,512]{1,0:T(8,128)}) custom-call(bf16[64,512]{1,0:T(8,128)(2,1)} %tok.1, bf16[448,512]{1,0:T(8,128)(2,1)} %bitcast.7, bf16[448,512]{1,0:T(8,128)(2,1)} %bitcast.8, bf16[448,512]{1,0:T(8,128)(2,1)} %dw.1, ...), custom_call_target="tpu_custom_call" | custom-call | flops 8999999488 | bytes 8388608 | tf_op jit(solution)/shard_map/sublayer/pallas_call | solution.py:418
  95.6 0.0 copy-start.2
  95.6 1.5 %copy.18 = bf16[64,512]{1,0:T(8,128)(2,1)} copy(bf16[64,512]{1,0:T(8,128)(2,1)} %get-tuple-element.20) | data formatting | bytes 131072
  97.1 0.0 copy-done.2
  97.1 0.6 copy.19
  97.8 0.0 copy-start.1
  97.8 2.2 %copy.20 = f32[512,448]{0,1:T(8,128)} copy(f32[512,448]{0,1:T(8,128)} %bitcast.6) | data formatting | bytes 1835008
  100.0 0.0 copy-done.1
  100.0 0.0 copy-start
  100.0 0.9 copy.21
  100.9 0.6 copy-done
  101.5 0.9 copy.22
Async XLA Ops:
  95.6 1.5 %copy-start.2 = (bf16[64,512]{1,0:T(8,128)(2,1)S(1)}, bf16[64,512]{1,0:T(8,128)(2,1)}, u32[]{:S(2)}) copy-start(bf16[64,512]{1,0:T(8,128)(2,1)} %get-tuple-element.21) | copy-start | bytes 196612
  97.8 2.2 %copy-start.1 = (f32[448,512]{1,0:T(8,128)S(1)}, f32[448,512]{1,0:T(8,128)}, u32[]{:S(2)}) copy-start(f32[448,512]{1,0:T(8,128)} %get-tuple-element.13) | copy-start | bytes 2752516
  100.0 1.5 %copy-start = (f32[448,512]{1,0:T(8,128)S(1)}, f32[448,512]{1,0:T(8,128)}, u32[]{:S(2)}) copy-start(f32[448,512]{1,0:T(8,128)} %get-tuple-element.24) | copy-start | bytes 2752516
